TPU v7x, 256 devices: a whole 4x4x8 slice. The times are simulated.
256 devices in a mesh: dp: 64 (over y_lo, z, x), tensor: 4 (over y_hi, core).
Axes of the slice: x: 4, y: 4 (y_hi: 2, y_lo: 2; y = y_hi * 2 + y_lo), z: 8, core: 2. Of those that a mesh axis runs over, the one named last changes fastest.
Arguments:
- gradient: bfloat16 [16384, 8192], P('tensor', 'dp'), may hold values from -6 to 6
- first_moment: float32 [16384, 8192], P('tensor', 'dp'), may hold values from -6 to 6
- second_moment: float32 [16384, 8192], P('tensor', 'dp'), may hold values from 0.05 to 2
- left_candidates: bfloat16 [64, 4, 1024, 1024], P('dp', 'tensor'), may hold values from -0.1875 to 0.1875
- right_candidates: bfloat16 [64, 4, 512, 512], P('dp', 'tensor'), may hold values from -0.25 to 0.25
- left_owner: int32 [8], replicated, may hold values from 0 to 31
- right_owner: int32 [4, 8], P('tensor'), may hold values from 0 to 63, as said below
Outputs:
- moment_new: float32 [16384, 8192], P('tensor', 'dp')
- second_new: float32 [16384, 8192], P('tensor', 'dp')
- update: bfloat16 [16384, 8192], P('tensor', 'dp')
Inputs may be any that keep to these rules, and one draw needn't show every extreme that they name: `right_owner`: each row holds 8 distinct dp indices; 0 and 64 - 1 are among them.
All inputs are finite; a program needn't handle non-finite values.
Results may differ from a plain program's by a relative error of at most 0.007.
Values may be sent and summed in bfloat16 or wider, within the bound.
A program may use at most 128 MiB of HBM per device.

v0:
```python
import jax
import jax.numpy as jnp
from jax import lax
from jax.sharding import PartitionSpec as P

beta_first = 0.9
beta_second = 0.95
correct_first = 1.0 - 0.9**10
correct_second = 1.0 - 0.95**10
epsilon = 1e-08


def spread(value, axis, root):
    mine = lax.axis_index(axis) == root
    return lax.psum(jnp.where(mine, value, jnp.zeros_like(value)), axis)


def partner(value, axis, distance):
    return lax.ppermute(value, axis, [(i, i ^ 1 << distance) for i in range(lax.axis_size(axis))])


def left_turn(columns, left_bases):
    column_rows = columns.shape[0]
    count_left, width_left = (left_bases.shape[0], left_bases.shape[1])
    blocks = columns.reshape(column_rows, count_left, width_left)
    rotated = jnp.einsum("cik,ikl->cil", blocks, left_bases, preferred_element_type=jnp.float32)
    return rotated.reshape(column_rows, count_left * width_left)


def left_back(step, left_bases):
    column_rows = step.shape[0]
    count_left, width_left = (left_bases.shape[0], left_bases.shape[1])
    blocks = step.reshape(column_rows, count_left, width_left)
    image = jnp.einsum("cil,ikl->cik", blocks, left_bases, preferred_element_type=jnp.float32)
    return image.reshape(column_rows, count_left * width_left).astype(jnp.bfloat16)


def adam_step(g_rot, m_rot, second_moment):
    second_new = beta_second * second_moment + (1.0 - beta_second) * g_rot * g_rot
    step = (m_rot / correct_first / (jnp.sqrt(second_new / correct_second) + epsilon)).astype(
        jnp.bfloat16
    )
    return (second_new, step)


def body(
    gradient,
    first_moment,
    second_moment,
    left_candidates,
    right_candidates,
    left_owner,
    right_owner,
):
    local_rows, strip_width = gradient.shape
    block_right = right_candidates.shape[2]
    count_right = local_rows // block_right
    width_left = left_candidates.shape[2]
    count_left = left_owner.shape[0]
    group_size = width_left // strip_width
    group_bits = group_size.bit_length() - 1
    tensor_count = lax.axis_size("tensor")
    dp_position = lax.axis_index("dp")
    group_place = dp_position % group_size
    moment_new = beta_first * first_moment + (1.0 - beta_first) * gradient.astype(jnp.float32)
    right_list = []
    for position in range(count_right):
        right_list.append(spread(right_candidates[0, 0], "dp", right_owner[0, position]))
    right_bases = jnp.stack(right_list)
    group_number = dp_position // group_size
    owner = left_owner[group_number]
    received = spread(left_candidates[0, 0], "tensor", owner % tensor_count)
    held = jnp.where(group_place == owner // tensor_count, received, jnp.zeros_like(received))
    for bit in range(group_bits):
        held = held + partner(held, "dp", bit)
    stacked = jnp.stack([gradient, moment_new.astype(jnp.bfloat16)]).reshape(
        2, count_right, block_right, strip_width
    )
    turned = jnp.einsum("jpq,sjpd->sjqd", right_bases, stacked, preferred_element_type=jnp.float32)
    turned = turned.astype(jnp.bfloat16).reshape(2, local_rows, strip_width)
    share_rows = width_left // group_size
    share = lax.dynamic_slice_in_dim(held, group_place * share_rows, share_rows, 0)
    every_left = lax.all_gather(share, "dp", axis=0, tiled=True)
    left_bases = every_left.reshape(count_left, width_left, width_left)
    columns = lax.all_to_all(turned, "dp", split_axis=1, concat_axis=2, tiled=True)
    g_rot = left_turn(columns[0], left_bases)
    m_rot = left_turn(columns[1], left_bases)
    rotated = jnp.stack([g_rot, m_rot])
    back = lax.all_to_all(rotated, "dp", split_axis=2, concat_axis=1, tiled=True)
    second_new, step = adam_step(back[0], back[1], second_moment)
    step_cols = lax.all_to_all(step, "dp", split_axis=0, concat_axis=1, tiled=True)
    image = left_back(step_cols, left_bases)
    image_rows = lax.all_to_all(image, "dp", split_axis=1, concat_axis=0, tiled=True)
    image_blocks = image_rows.reshape(count_right, block_right, strip_width)
    update = jnp.einsum(
        "jpq,jqd->jpd", right_bases, image_blocks, preferred_element_type=jnp.float32
    )
    update = update.astype(jnp.bfloat16).reshape(local_rows, strip_width)
    return (moment_new, second_new, update)


def solution(mesh):
    placed = (
        P("tensor", "dp"),
        P("tensor", "dp"),
        P("tensor", "dp"),
        P("dp", "tensor", None, None),
        P("dp", "tensor", None, None),
        P(),
        P("tensor", None),
    )
    return jax.shard_map(
        body,
        mesh=mesh,
        in_specs=placed,
        out_specs=(P("tensor", "dp"), P("tensor", "dp"), P("tensor", "dp")),
        check_vma=False,
    )
```

profile of v0, /device:TPU:6, one launch (start us, length us, event | category | flops | bytes accessed | tf_op | source)
XLA Modules:
  0.0 1334.0 jit_solution(15589584506030546533)
XLA Ops:
  13.5 67.4 %all-reduce.4.cloned.1.call-done = bf16[1024,1024]{1,0:T(8,128)(2,1)} async-done(((bf16[1024,1024]{1,0:T(8,128)(2,1)}), bf16[1024,1024]{1,0:T(8,128)(2,1)}) %all-reduce.4.cloned.1.call-update) | async-done | bytes 2097168 | tf_op jit(solution)/shard_map/psum | solution.py:15
  87.7 41.2 %collective-permute-done = bf16[1024,1024]{1,0:T(8,128)(2,1)} collective-permute-done((bf16[1024,1024]{1,0:T(8,128)(2,1)S(1)}, bf16[1024,1024]{1,0:T(8,128)(2,1)}, u32[]{:S(2)}, u32[]{:S(2)}) %collective-permute-start) | collective-permute-done | bytes 2097184 | tf_op jit(solution)/shard_map/ppermute | solution.py:19
  128.9 1.8 fusion.26
  132.3 2.0 select_bitcast_fusion.1
  134.4 52.3 %collective-permute-done.1 = bf16[1024,1024]{1,0:T(8,128)(2,1)} collective-permute-done((bf16[1024,1024]{1,0:T(8,128)(2,1)S(1)}, bf16[1024,1024]{1,0:T(8,128)(2,1)}, u32[]{:S(2)}, u32[]{:S(2)}) %collective-permute-start.1) | collective-permute-done | bytes 2097184 | tf_op jit(solution)/shard_map/ppermute | solution.py:19
  186.7 3.9 add.59
  190.6 3.1 collective-permute-start.2
  193.8 52.7 %collective-permute-done.2 = bf16[1024,1024]{1,0:T(8,128)(2,1)S(1)} collective-permute-done((bf16[1024,1024]{1,0:T(8,128)(2,1)}, bf16[1024,1024]{1,0:T(8,128)(2,1)S(1)}, u32[]{:S(2)}, u32[]{:S(2)}) %collective-permute-start.2) | collective-permute-done | bytes 2097184 | tf_op jit(solution)/shard_map/ppermute | solution.py:19
  246.5 1.8 dynamic-slice_add_fusion
  248.3 3.3 fusion.17
  252.7 498.6 %all-reduce.6.cloned.1.call-done = (bf16[1,512,512]{2,1,0:T(8,128)(2,1)}, bf16[1,512,512]{2,1,0:T(8,128)(2,1)}, bf16[1,512,512]{2,1,0:T(8,128)(2,1)}, bf16[1,512...) async-done(((bf16[1,512,512]{2,1,0:T(8,128)(2,1)}, ...) | async-done | bytes 4194320 | tf_op jit(solution)/shard_map/psum | solution.py:15
  754.9 2.0 copy-done.9
  756.9 2.6 convert_bitcast_fusion
  759.5 3.0 copy.38
  762.5 17.8 %copy.39 = bf16[2,4096,128]{2,0,1:T(2,128)(2,1)S(1)} copy(bf16[2,4096,128]{2,1,0:T(8,128)(2,1)S(1)} %bitcast.83) | data formatting | bytes 4194304 | tf_op jit(solution)/shard_map/reshape | solution.py:80
  780.4 57.6 %all_to_all.59 = bf16[2,4096,128]{2,0,1:T(2,128)(2,1)S(1)} all-to-all(bf16[2,4096,128]{2,0,1:T(2,128)(2,1)S(1)} %copy.39), channel_id=1, replica_groups=mesh['dp'=64,'tensor'=4] {'dp'}, dimensions={1} | all-to-all | bytes 4194304 | tf_op jit(solution)/shard_map/all_to_all | solution.py:85
  840.5 253.5 %all-gather.2.cloned.1.call-done = bf16[8192,1024]{1,0:T(8,128)(2,1)} async-done(((bf16[128,1024]{1,0:T(8,128)(2,1)}), bf16[8192,1024]{1,0:T(8,128)(2,1)}) %all-gather.2.cloned.1.call-update) | async-done | bytes 16777232 | tf_op jit(solution)/shard_map/all_gather | solution.py:83
  1094.0 9.3 convolution_bitcast_fusion
  1106.0 9.3 convolution_bitcast_fusion.1
  1118.0 4.6 pad_maximum_fusion
  1122.6 10.8 copy.45
  1133.4 11.6 reshape.88
  1145.0 70.6 %all_to_all.60 = f32[64,1,16384]{2,1,0:T(1,128)} all-to-all(f32[64,1,16384]{2,1,0:T(1,128)} %reshape.88), channel_id=1, replica_groups=mesh['dp'=64,'tensor'=4] {'dp'}, dimensions={0} | all-to-all | bytes 8388608 | tf_op jit(solution)/shard_map/all_to_all | solution.py:89
  1216.1 13.7 %reduce = f32[64,16384]{1,0:T(8,128)} reduce(f32[64,1,16384]{2,1,0:T(1,128)} %all_to_all.60, f32[]{:T(128)} %broadcast.60), dimensions={1}, to_apply=%all_to_all.47.reduce_sub_computation | reduce | bytes 8388612 | tf_op jit(solution)/shard_map/all_to_all | solution.py:89
  1229.8 9.2 reshape.89
  1239.0 8.6 copy.54
  1247.6 3.0 fusion.18
  1253.4 2.4 fusion.6
  1255.8 31.7 %all_to_all.61 = bf16[64,64,128]{2,1,0:T(8,128)(2,1)S(1)} all-to-all(bf16[64,64,128]{2,1,0:T(8,128)(2,1)S(1)} %bitcast.85), channel_id=1, replica_groups=mesh['dp'=64,'tensor'=4] {'dp'}, dimensions={0} | all-to-all | bytes 2097152 | tf_op jit(solution)/shard_map/all_to_all | solution.py:91
  1288.8 8.9 fusion.11
  1299.5 24.6 %all_to_all.62 = bf16[64,64,128]{2,0,1:T(8,128)(2,1)S(1)} all-to-all(bf16[64,64,128]{2,0,1:T(8,128)(2,1)S(1)} %copy.52), channel_id=1, replica_groups=mesh['dp'=64,'tensor'=4] {'dp'}, dimensions={1} | all-to-all | bytes 2097152 | tf_op jit(solution)/shard_map/all_to_all | solution.py:93
  1324.1 2.2 convolution_convert_fusion
  (61 shorter events, 25.0 us)
Async XLA Ops:
  8.0 72.9 %all-reduce.4.cloned.1.call-start = ((), (), s32[]{:S(2)}) async-start(), calls=%async_computation.4 | async-start | bytes 4194304 | tf_op jit(solution)/shard_map/psum | solution.py:15
  12.8 738.6 %all-reduce.6.cloned.1.call-start = ((), (), s32[]{:S(2)}) async-start(), calls=%async_computation.6 | async-start | bytes 8388608 | tf_op jit(solution)/shard_map/psum | solution.py:15
  13.5 68.5 %copy-start.11 = (s32[1,8]{1,0:T(1,128)S(1)}, s32[1,8]{1,0:T(1,128)}, u32[]{:S(2)}) copy-start(s32[1,8]{1,0:T(1,128)} %param.13) | copy-start | bytes 100
  81.0 47.9 %collective-permute-start = (bf16[1024,1024]{1,0:T(8,128)(2,1)S(1)}, bf16[1024,1024]{1,0:T(8,128)(2,1)}, u32[]{:S(2)}, u32[]{:S(2)}) collective-permute-start(bf16[1024,1024]{1,0:T(8,128)(2,1)S(1)} %broadcast_select_fusion), channel_id=1, source_target_pairs={{0,4},{4,0},{8,12},{12,8},{16,20},{20,16},{24,28},{28,24},{32,36},... | collective-permute-start | bytes 6291464 | tf_op jit(solution)/shard_map/ppermute | solution.py:19
  87.7 44.6 %copy-start.8 = (bf16[1,1,512,512]{3,2,1,0:T(8,128)(2,1)S(1)}, bf16[1,1,512,512]{3,2,1,0:T(8,128)(2,1)}, u32[]{:S(2)}) copy-start(bf16[1,1,512,512]{3,2,1,0:T(8,128)(2,1)} %param.11) | copy-start | bytes 1572868
  130.8 56.0 %collective-permute-start.1 = (bf16[1024,1024]{1,0:T(8,128)(2,1)S(1)}, bf16[1024,1024]{1,0:T(8,128)(2,1)}, u32[]{:S(2)}, u32[]{:S(2)}) collective-permute-start(bf16[1024,1024]{1,0:T(8,128)(2,1)S(1)} %fusion.26), channel_id=1, source_target_pairs={{0,8},{4,12},{8,0},{12,4},{16,24},{20,28},{24,16},{28,20},{32,40},... | collective-permute-start | bytes 6291464 | tf_op jit(solution)/shard_map/ppermute | solution.py:19
  134.4 113.9 %copy-start = (bf16[4096,128]{1,0:T(8,128)(2,1)S(1)}, bf16[4096,128]{1,0:T(8,128)(2,1)}, u32[]{:S(2)}) copy-start(bf16[4096,128]{1,0:T(8,128)(2,1)} %param.7) | copy-start | bytes 3145732
  134.4 959.6 %all-gather.2.cloned.1.call-start = ((), (), s32[]{:S(2)}) async-start(), calls=%async_computation.5 | async-start | bytes 17039360 | tf_op jit(solution)/shard_map/all_gather | solution.py:83
  190.6 55.9 %collective-permute-start.2 = (bf16[1024,1024]{1,0:T(8,128)(2,1)}, bf16[1024,1024]{1,0:T(8,128)(2,1)S(1)}, u32[]{:S(2)}, u32[]{:S(2)}) collective-permute-start(bf16[1024,1024]{1,0:T(8,128)(2,1)} %add.59), channel_id=1, source_target_pairs={{0,16},{4,20},{8,24},{12,28},{16,0},{20,4},{24,8},{28,12},{32,48},... | collective-permute-start | bytes 6291464 | tf_op jit(solution)/shard_map/ppermute | solution.py:19
  751.3 2.4 copy-start.7
  751.3 2.4 copy-start.6
  751.3 2.5 copy-start.5
  752.5 1.3 copy-start.4
  753.7 1.1 copy-start.3
  753.7 1.2 copy-start.2
  754.9 2.0 copy-start.9
  1251.8 1.6 copy-start.1
  1298.8 25.3 %copy-start.10 = (bf16[8,512,512]{2,1,0:T(8,128)(2,1)S(1)}, bf16[8,512,512]{2,1,0:T(8,128)(2,1)}, u32[]{:S(2)}) copy-start(bf16[8,512,512]{2,1,0:T(8,128)(2,1)} %copy-done.9) | copy-start | bytes 12582916
Sparse Core Ops, SparseCore 0:
  12.9 67.9 all-reduce.3
Sparse Core Ops, SparseCore 1:
  134.4 616.8 all-reduce.5
  753.0 340.9 all-gather.1
where the time goes:
time: 1340 us; the launch traced here: 1330 us
  waiting for transfers between devices  966 us (72%)
  blocking collectives  185 us (14%)
  local copies, waits for them, and re-layouts  83.9 us (6%)
  other arithmetic  38 us (3%)
  matrix products  32.3 us (2%)
  between operations  23.8 us (2%)
    psum x2, waiting for transfers between devices, spread(): return lax.psum(jnp.where(mine, value, jnp.zeros_like(value)), axis)  566 us
    all_gather x1, waiting for transfers between devices, body(): every_left = lax.all_gather(share, 'dp', axis=0, tiled=True)  253 us
    ppermute x3, waiting for transfers between devices, partner(): lax.ppermute(value, axis, [(i, i ^ 1 << distance) for i in range(lax.axis...  146 us
    all_to_all x1, blocking collectives, body(): lax.all_to_all(rotated, 'dp', split_axis=2, concat_axis=1, tiled=True)  70.6 us
    all_to_all x1, blocking collectives, body(): lax.all_to_all(turned, 'dp', split_axis=1, concat_axis=2, tiled=True)  57.6 us
    all_to_all x1, blocking collectives, body(): lax.all_to_all(step, 'dp', split_axis=0, concat_axis=1, tiled=True)  31.7 us
  transfers between devices with their start and end apart: 6, of which 6 were waited for; matrix products, arithmetic and copies ran while one was open for 3% of the time, Pallas kernels for 0%

commit v1 on v0

v1 whole, which is shorter than its diff:
```python
import jax
import jax.numpy as jnp
from jax import lax
from jax.experimental import pallas as pl
from jax.experimental.pallas import tpu as pltpu
from jax.sharding import PartitionSpec as P

MESH = pl.DeviceIdType.MESH
beta_first = 0.9
beta_second = 0.95
correct_first = 1.0 - 0.9**10
correct_second = 1.0 - 0.95**10
epsilon = 1e-08


def flip4(x, a):
    if a == 0:
        return x
    if a == 1:
        return x + 1 - 2 * (x % 2)
    if a == 2:
        return (x + 2) % 4
    return 3 - x


def kernel(
    grad, first, second, lcand, rcand, lown, rown,
    grot_out, upd_out,
    g_strip, f_strip, s_strip, m_send, s_send,
    g_in, m_in, s_in,
    l_core, l_half, l_y, l_quar, l_x, l_z, l_all,
    r_one, r_slot, r_pair, r_half, r_ring, r_part, r_cols, r_all,
    t_g, t_m, gsq, stp, g_send, u_send,
    send_sem, recv_sem, load_sem,
):
    dp, tn = lax.axis_index("dp"), lax.axis_index("tensor")
    ylo, z, x = dp // 32, (dp // 4) % 8, dp % 4
    yhi, core = tn // 2, tn % 2
    zlo = z % 2
    p = zlo * 4 + x
    group = dp // 8

    def dev(ylo_=None, z_=None, x_=None, yhi_=None, core_=None):
        a = ylo if ylo_ is None else ylo_
        b = z if z_ is None else z_
        c = x if x_ is None else x_
        d = yhi if yhi_ is None else yhi_
        e = core if core_ is None else core_
        return (a * 32 + b * 4 + c, d * 2 + e)

    zpair = z + 1 - 2 * zlo

    def in_group(r):
        return dev(x_=flip4(x, r % 4), z_=zpair if r >= 4 else z)

    def group_place(r):
        return (1 - zlo if r >= 4 else zlo) * 4 + flip4(x, r % 4)

    def in_plane(r):
        return dev(x_=flip4(x, r % 4), ylo_=1 - ylo if r >= 4 else ylo)

    def plane_place(r):
        return (1 - ylo if r >= 4 else ylo) * 4 + flip4(x, r % 4)

    count = [0]

    def remote(src, dst, to):
        i = count[0]
        count[0] += 1
        c = pltpu.make_async_remote_copy(
            src_ref=src, dst_ref=dst, send_sem=send_sem.at[i], recv_sem=recv_sem.at[i],
            device_id=to, device_id_type=MESH,
        )
        c.start()
        return c

    lcount = [0]

    def local(src, dst):
        c = pltpu.make_async_copy(src, dst, load_sem.at[lcount[0]])
        lcount[0] += 1
        c.start()
        return c

    sent = []

    def arrive(copies):
        for c in copies:
            c.wait_recv()
        sent.extend(copies)

    ld_r = local(
        rcand.at[0, 0, pl.ds(pl.multiple_of((x % 2) * 256, 256), 256),
                 pl.ds(pl.multiple_of((ylo * 2 + x // 2) * 128, 128), 128)],
        r_one.at[ylo * 4 + x],
    )
    ld_l = [
        local(lcand.at[0, 0, :, pl.ds(pl.multiple_of((core * 4 + j) * 128, 128), 128)], l_core.at[core, j])
        for j in range(4)
    ]
    ld_g0 = local(grad.at[pl.ds(pl.multiple_of(p * 512, 512), 512)], g_in.at[p])
    ld_g, ld_f, ld_s = local(grad, g_strip), local(first, f_strip), local(second, s_strip)

    peers = [in_group(r) for r in range(1, 8)]
    peers += [in_plane(r) for r in range(4, 8)]
    peers += [dev(z_=(z + r) % 8) for r in range(2, 7)]
    peers += [dev(z_=(z + 7 + 2 * zlo) % 8)]
    peers += [dev(yhi_=1 - yhi), dev(core_=1 - core)]
    barrier = pltpu.get_barrier_semaphore()
    for to in peers:
        pl.semaphore_signal(barrier, inc=1, device_id=to, device_id_type=MESH)
    pl.semaphore_wait(barrier, len(peers))

    lo = lown[group]
    o_core, o_yhi, o_x, o_zlo = lo % 2, (lo // 2) % 2, (lo // 4) % 4, lo // 16

    def right(slot):
        d = rown[0, (slot % 2) * 4 + slot // 2]
        return d // 32, (d // 4) % 8, d % 4

    l1 = [
        remote(
            lcand.at[0, 0, :, pl.ds(pl.multiple_of(((1 - core) * 4 + j) * 128, 128), 128)],
            l_core.at[core, j], dev(core_=1 - core),
        )
        for j in range(4)
    ]
    r1 = []
    for r in range(1, 8):
        q = plane_place(r)
        r1.append(remote(
            rcand.at[0, 0, pl.ds(pl.multiple_of((q % 2) * 256, 256), 256),
                     pl.ds(pl.multiple_of((q // 2) * 128, 128), 128)],
            r_one.at[ylo * 4 + x], in_plane(r),
        ))

    def spread(src, dst):
        out = []
        for r in range(1, 8):
            q = group_place(r)
            out.append(remote(src.at[pl.ds(pl.multiple_of(q * 512, 512), 512)], dst.at[p], in_group(r)))
        return out

    a_g = spread(grad, g_in)

    for c in ld_l:
        c.wait()
    arrive(l1)
    l_half[...] = l_core[o_core]
    l2 = [remote(l_half.at[pl.ds((1 - yhi) * 2, 2)], l_y.at[yhi], dev(yhi_=1 - yhi))]
    l_y[yhi] = l_half[pl.ds(yhi * 2, 2)]

    ld_g.wait()
    ld_f.wait()

    def fold(i, carry):
        rows = pl.ds(pl.multiple_of(i * 256, 256), 256)
        m_send[rows] = (
            beta_first * f_strip[rows] + (1.0 - beta_first) * g_strip[rows].astype(jnp.float32)
        ).astype(jnp.bfloat16)
        return carry

    lax.fori_loop(0, 16, fold, 0)
    a_m = spread(m_send, m_in)
    m_in[p] = m_send[pl.ds(pl.multiple_of(p * 512, 512), 512)]

    ld_r.wait()
    arrive(r1)
    for s in range(8):
        oy, oz, ox = right(s)
        r_slot[s] = r_one[oy * 4 + ox]
    r2 = [remote(
        r_slot.at[:, pl.ds(pl.multiple_of((1 - zlo) * 128, 128), 128)], r_pair.at[zlo],
        dev(z_=(z + 7 + 2 * zlo) % 8),
    )]
    r_pair[zlo] = r_slot[:, pl.ds(pl.multiple_of(zlo * 128, 128), 128)]

    ld_s.wait()

    def narrow(i, carry):
        rows = pl.ds(pl.multiple_of(i * 256, 256), 256)
        s_send[rows] = s_strip[rows].astype(jnp.bfloat16)
        return carry

    lax.fori_loop(0, 16, narrow, 0)
    s_in[p] = s_send[pl.ds(pl.multiple_of(p * 512, 512), 512)]

    arrive(r2)
    for s in range(8):
        oy, oz, ox = right(s)
        r_half[s] = r_pair[oz % 2, s]
    ring = ((z + 1) // 2) % 4
    r3 = [
        remote(
            r_half.at[:, pl.ds(pl.multiple_of(((ring + r) % 4) * 32, 32), 32)], r_ring.at[ring],
            dev(z_=(z + 2 * r) % 8),
        )
        for r in range(1, 4)
    ]
    r_ring[ring] = r_half[:, pl.ds(pl.multiple_of(ring * 32, 32), 32)]

    arrive(l2)
    for i in range(4):
        l_quar[i] = l_y[o_yhi, i // 2, (i % 2) * 512:(i % 2) * 512 + 512]
    l3 = [remote(l_quar.at[flip4(x, r)], l_x.at[x], dev(x_=flip4(x, r))) for r in range(1, 4)]
    l_x[x] = l_quar[x]

    arrive(r3)
    for s in range(8):
        oy, oz, ox = right(s)
        r_part[s // 2, s % 2] = r_ring[((oz + 1) // 2) % 4, s]
    r4 = [remote(r_part.at[flip4(x, r)], r_cols.at[x], dev(x_=flip4(x, r))) for r in range(1, 4)]
    r_cols[x] = r_part[x]

    a_s = spread(s_send, s_in)

    arrive(r4)
    sub = zlo * 4 + ring
    r5 = [
        remote(
            r_cols.at[:, (z + r) % 2], r_all.at[pl.ds(ylo * 4, 4), sub], dev(z_=(z + r) % 8),
        )
        for r in range(1, 8)
    ]
    r_all[pl.ds(ylo * 4, 4), sub] = r_cols[:, zlo]

    arrive(l3)
    l_z[zlo] = l_x[o_x]
    l4 = [remote(l_z.at[zlo], l_z.at[zlo], dev(z_=zpair))]
    arrive(l4)
    place = core * 8 + yhi * 4 + x
    l_all[place] = l_z[o_zlo]
    l5 = [remote(l_all.at[place], l_all.at[place], dev(x_=flip4(x, r))) for r in range(1, 4)]

    arrive(r5)
    r6 = [remote(r_all.at[pl.ds(ylo * 4, 4)], r_all.at[pl.ds(ylo * 4, 4)], dev(ylo_=1 - ylo))]

    arrive(l5)
    mine = pl.ds(core * 8 + yhi * 4, 4)
    l6 = [remote(l_all.at[mine], l_all.at[mine], dev(yhi_=1 - yhi))]

    arrive(r6)

    def right_basis():
        return jnp.concatenate([r_all[2 * j:2 * j + 2].reshape(512, 128) for j in range(4)], axis=1)

    def turn(src, dst):
        basis = right_basis()

        def one(j, carry):
            cols = jnp.concatenate([src[2 * j], src[2 * j + 1]], axis=1)
            t = lax.dot_general(basis, cols, (((0,), (0,)), ((), ())), preferred_element_type=jnp.float32)
            dst[:, pl.ds(pl.multiple_of(j * 256, 256), 256)] = t.astype(jnp.bfloat16)
            return carry

        lax.fori_loop(0, 4, one, 0)

    ld_g0.wait()
    arrive(a_g)
    turn(g_in, t_g)
    arrive(a_m)
    turn(m_in, t_m)

    arrive(l6)
    l7 = [remote(l_all.at[pl.ds(core * 8, 8)], l_all.at[pl.ds(core * 8, 8)], dev(core_=1 - core))]
    arrive(l7)

    def pair_at(s):
        return (1 - zlo if s >= 2 else zlo) * 2 + (1 - x // 2 if s % 2 else x // 2)

    def left_cols(j):
        return jnp.concatenate(
            [l_all[pl.ds(4 * j, 2)].reshape(1024, 128), l_all[pl.ds(4 * j + 2, 2)].reshape(1024, 128)], axis=1
        )

    home = pl.ds(pl.multiple_of(p * 512, 512), 512)
    back = []

    def send_home(buf, out, s):
        for r in (2 * s, 2 * s + 1):
            q = group_place(r)
            if r == 0:
                back_local.append(local(buf.at[q], out.at[home]))
            else:
                back.append(remote(buf.at[q], out.at[home], in_group(r)))

    back_local = []
    for s in range(4):
        j = pair_at(s)
        g = jnp.dot(t_g[...], left_cols(j), preferred_element_type=jnp.float32)
        gsq[j] = g * g
        low = g.astype(jnp.bfloat16)
        g_send[2 * j] = low[:, :128]
        g_send[2 * j + 1] = low[:, 128:]
        send_home(g_send, grot_out, s)

    arrive(a_s)

    def left_moment(j, carry):
        m = jnp.dot(t_m[...], left_cols(j), preferred_element_type=jnp.float32)
        old = jnp.concatenate([s_in[2 * j], s_in[2 * j + 1]], axis=1).astype(jnp.float32)
        new = beta_second * old + (1.0 - beta_second) * gsq[j]
        step = m / (correct_first * (jnp.sqrt(new * (1.0 / correct_second)) + epsilon))
        stp[:, pl.ds(pl.multiple_of(j * 256, 256), 256)] = step.astype(jnp.bfloat16)
        return carry

    lax.fori_loop(0, 4, left_moment, 0)

    for s in range(4):
        j = pair_at(s)
        half = j // 2
        start = pl.ds(pl.multiple_of((j % 2) * 256, 256), 256)
        rows = jnp.concatenate([l_all[2 * b + half, start] for b in range(8)], axis=1)
        image = lax.dot_general(
            stp[...], rows, (((1,), (1,)), ((), ())), preferred_element_type=jnp.float32
        ).astype(jnp.bfloat16)
        out = jnp.dot(right_basis(), image, preferred_element_type=jnp.float32).astype(jnp.bfloat16)
        u_send[2 * j] = out[:, :128]
        u_send[2 * j + 1] = out[:, 128:]
        send_home(u_send, upd_out, s)

    arrive(back)
    for c in back_local:
        c.wait()
    for c in sent:
        c.wait_send()


def body(gradient, first_moment, second_moment, left_candidates, right_candidates, left_owner, right_owner):
    bf, f32 = jnp.bfloat16, jnp.float32
    any_, smem = pl.BlockSpec(memory_space=pl.ANY), pl.BlockSpec(memory_space=pltpu.SMEM)
    vm = pltpu.VMEM
    strip = jax.ShapeDtypeStruct(gradient.shape, bf)
    grot, update = pl.pallas_call(
        kernel,
        name="soap_swap",
        out_shape=(strip, strip),
        in_specs=[any_] * 5 + [smem] * 2,
        out_specs=(any_, any_),
        scratch_shapes=[
            vm((4096, 128), bf), vm((4096, 128), f32), vm((4096, 128), f32), vm((4096, 128), bf), vm((4096, 128), bf),
            vm((8, 512, 128), bf), vm((8, 512, 128), bf), vm((8, 512, 128), bf),
            vm((2, 4, 1024, 128), bf), vm((4, 1024, 128), bf), vm((2, 2, 1024, 128), bf),
            vm((4, 512, 128), bf), vm((4, 512, 128), bf), vm((2, 512, 128), bf), vm((16, 512, 128), bf),
            vm((8, 256, 128), bf), vm((8, 256, 128), bf), vm((2, 8, 128, 128), bf), vm((8, 128, 128), bf),
            vm((4, 8, 32, 128), bf), vm((4, 2, 32, 128), bf), vm((4, 2, 32, 128), bf), vm((8, 8, 32, 128), bf),
            vm((512, 1024), bf), vm((512, 1024), bf), vm((4, 512, 256), f32), vm((512, 1024), bf),
            vm((8, 512, 128), bf), vm((8, 512, 128), bf),
            pltpu.SemaphoreType.DMA((72,)), pltpu.SemaphoreType.DMA((72,)), pltpu.SemaphoreType.DMA((16,)),
        ],
        compiler_params=pltpu.CompilerParams(
            collective_id=0, has_side_effects=True, vmem_limit_bytes=56 * 2**20
        ),
    )(gradient, first_moment, second_moment, left_candidates, right_candidates, left_owner, right_owner)
    moment_new = beta_first * first_moment + (1.0 - beta_first) * gradient.astype(f32)
    turned = grot.astype(f32)
    second_new = beta_second * second_moment + (1.0 - beta_second) * turned * turned
    return moment_new, second_new, update


def solution(mesh):
    strips = P("tensor", "dp")
    placed = (strips, strips, strips, P("dp", "tensor", None, None), P("dp", "tensor", None, None), P(), P("tensor", None))
    return jax.shard_map(body, mesh=mesh, in_specs=placed, out_specs=(strips,) * 3, check_vma=False)
```

time: 1340 us -> 120 us (0.09)
  the two profiles are of different devices: /device:TPU:6 before, /device:TPU:1 now
where the time goes in v1:
time: 120 us
  Pallas kernels  114 us (95%)
  other arithmetic  3.93 us (3%)
    pallas_call x1, Pallas kernels, body(): pl.pallas_call(kernel, name='soap_swap', out_shape=(strip, strip), in_spe...  114 us
    add x1, other arithmetic, body(): beta_second * second_moment + (1.0 - beta_second) * turned * turned  3.93 us

profile of v1, /device:TPU:1, one launch (start us, length us, event | category | flops | bytes accessed | tf_op | source)
XLA Modules:
  0.0 119.9 jit_solution(13811496403546214664)
XLA Ops:
  0.6 0.0 copy-start.1
  0.6 0.0 copy-start
  0.7 0.0 copy-start.2
  0.7 114.3 %soap_swap.1 = (bf16[4096,128]{1,0:T(8,128)(2,1)}, bf16[4096,128]{1,0:T(8,128)(2,1)}) custom-call(bf16[4096,128]{1,0:T(8,128)(2,1)} %grad.1, f32[4096,128]{1,0:T(8,128)} %first.1, f32[4096,128]{1,0:T(8,128)} %second.1, bf16[1,1,1024,1024]{3,2,1,0:T(8,128)(2,1)} %lcand.1, bf16[1,1,512,512]{3,2,1,0:T(8,128)(2,1)} %rcand.1, s32[8]{0:T(128)} %lown.1, s32[1,8]{1,0:T(1,128)} %rown.1), custom_call_target="tpu_custom_call" | custom-call | tf_op jit(solution)/shard_map/soap_swap/pallas_call | solution.py:334
  115.0 0.0 copy-done.1
  115.0 0.0 copy-done
  115.0 0.0 copy-done.2
  115.0 0.0 copy-start.3
  115.0 3.9 %fusion = (f32[4096,128]{1,0:T(8,128)}, f32[4096,128]{1,0:T(8,128)}) fusion(bf16[4096,128]{1,0:T(8,128)(2,1)} %get-tuple-element.5, f32[4096,128]{1,0:T(8,128)S(1)} %copy-done.1, bf16[4096,128]{1,0:T(8,128)(2,1)S(1)} %copy-done.2, f32[4096,128]{1,0:T(8,128)S(1)} %copy-done), kind=kLoop, calls=%fused_computation.1 | loop fusion | flops 4718592 | bytes 10485760 | tf_op jit(solution)/shard_map/add | solution.py:357
  118.9 0.0 copy-done.3
  118.9 1.0 copy.11
Async XLA Ops:
  0.6 114.3 %copy-start.1 = (f32[4096,128]{1,0:T(8,128)S(1)}, f32[4096,128]{1,0:T(8,128)}, u32[]{:S(2)}) copy-start(f32[4096,128]{1,0:T(8,128)} %second.1) | copy-start | bytes 6291460
  0.6 114.3 %copy-start = (f32[4096,128]{1,0:T(8,128)S(1)}, f32[4096,128]{1,0:T(8,128)}, u32[]{:S(2)}) copy-start(f32[4096,128]{1,0:T(8,128)} %first.1) | copy-start | bytes 6291460
  0.7 114.3 %copy-start.2 = (bf16[4096,128]{1,0:T(8,128)(2,1)S(1)}, bf16[4096,128]{1,0:T(8,128)(2,1)}, u32[]{:S(2)}) copy-start(bf16[4096,128]{1,0:T(8,128)(2,1)} %grad.1) | copy-start | bytes 3145732
  115.0 3.9 %copy-start.3 = (bf16[4096,128]{1,0:T(8,128)(2,1)S(1)}, bf16[4096,128]{1,0:T(8,128)(2,1)}, u32[]{:S(2)}) copy-start(bf16[4096,128]{1,0:T(8,128)(2,1)} %get-tuple-element.14) | copy-start | bytes 3145732

commit v2 on v1

v2 whole, which is shorter than its diff:
```python
import jax
import jax.numpy as jnp
from jax import lax
from jax.experimental import pallas as pl
from jax.experimental.pallas import tpu as pltpu
from jax.sharding import PartitionSpec as P

MESH = pl.DeviceIdType.MESH
beta_first = 0.9
beta_second = 0.95
correct_first = 1.0 - 0.9**10
correct_second = 1.0 - 0.95**10
epsilon = 1e-08

ORDER = "PgBsQggmmPBggmAQPgABPQAmBPBAQPgABmQssmAsQsPsmsBAQABGhhhShMwuuuu"


def flip4(x, a):
    if a == 0:
        return x
    if a == 1:
        return x + 1 - 2 * (x % 2)
    if a == 2:
        return (x + 2) % 4
    return 3 - x


def kernel(
    grad, first, second, lcand, rcand, lown, rown,
    grot_out, upd_out,
    g_strip, f_strip, s_strip, m_send, s_send,
    g_in, m_in, s_in,
    l_half, l_quar, l_all, r_slot, r_half, r_part, r_cols, r_all,
    l_core0, l_core1, l_y0, l_y1, l_x0, l_x1, l_z0, l_z1, r_one0, r_one1, r_pair0, r_pair1, r_ring0, r_ring1,
    t_g, t_m, gsq, stp, g_send, u_send,
    send_sem, recv_sem, load_sem,
):
    dp, tn = lax.axis_index("dp"), lax.axis_index("tensor")
    ylo, z, x = dp // 32, (dp // 4) % 8, dp % 4
    yhi, core = tn // 2, tn % 2
    zlo = z % 2
    l_core, l_y, l_x, l_z = (l_core0, l_core1), (l_y0, l_y1), (l_x0, l_x1), (l_z0, l_z1)
    r_one, r_pair, r_ring = (r_one0, r_one1), (r_pair0, r_pair1), (r_ring0, r_ring1)
    p = zlo * 4 + x
    group = dp // 8

    def dev(ylo_=None, z_=None, x_=None, yhi_=None, core_=None):
        a = ylo if ylo_ is None else ylo_
        b = z if z_ is None else z_
        c = x if x_ is None else x_
        d = yhi if yhi_ is None else yhi_
        e = core if core_ is None else core_
        return (a * 32 + b * 4 + c, d * 2 + e)

    zpair = z + 1 - 2 * zlo

    def in_group(r):
        return dev(x_=flip4(x, r % 4), z_=zpair if r >= 4 else z)

    def group_place(r):
        return (1 - zlo if r >= 4 else zlo) * 4 + flip4(x, r % 4)

    def in_plane(r):
        return dev(x_=flip4(x, r % 4), ylo_=1 - ylo if r >= 4 else ylo)

    def plane_place(r):
        return (1 - ylo if r >= 4 else ylo) * 4 + flip4(x, r % 4)

    count = [0]

    def remote(src, dst, to):
        i = count[0]
        count[0] += 1
        c = pltpu.make_async_remote_copy(
            src_ref=src, dst_ref=dst, send_sem=send_sem.at[i], recv_sem=recv_sem.at[i],
            device_id=to, device_id_type=MESH,
        )
        c.start()
        return c

    lcount = [0]

    def local(src, dst):
        c = pltpu.make_async_copy(src, dst, load_sem.at[lcount[0]])
        lcount[0] += 1
        c.start()
        return c

    sent = []

    def arrive(copies):
        for c in copies:
            c.wait_recv()
        sent.extend(copies)

    ld_r = [
        local(
            rcand.at[0, 0, pl.ds(pl.multiple_of((x % 2) * 256 + h * 128, 128), 128),
                     pl.ds(pl.multiple_of((ylo * 2 + x // 2) * 128, 128), 128)],
            r_one[h].at[ylo * 4 + x],
        )
        for h in range(2)
    ]
    ld_l = [
        [
            local(
                lcand.at[0, 0, pl.ds(h * 512, 512), pl.ds(pl.multiple_of((core * 4 + j) * 128, 128), 128)],
                l_core[h].at[core, j],
            )
            for j in range(4)
        ]
        for h in range(2)
    ]
    ld_g0 = local(grad.at[pl.ds(pl.multiple_of(p * 512, 512), 512)], g_in.at[p])
    ld_g, ld_f, ld_s = local(grad, g_strip), local(first, f_strip), local(second, s_strip)

    peers = [in_group(r) for r in range(1, 8)]
    peers += [in_plane(r) for r in range(4, 8)]
    peers += [dev(z_=(z + r) % 8) for r in range(2, 7)]
    peers += [dev(z_=(z + 7 + 2 * zlo) % 8)]
    peers += [dev(yhi_=1 - yhi), dev(core_=1 - core)]
    barrier = pltpu.get_barrier_semaphore()
    for to in peers:
        pl.semaphore_signal(barrier, inc=1, device_id=to, device_id_type=MESH)
    pl.semaphore_wait(barrier, len(peers))

    lo = lown[group]
    o_core, o_yhi, o_x, o_zlo = lo % 2, (lo // 2) % 2, (lo // 4) % 4, lo // 16

    def right(slot):
        d = rown[0, (slot % 2) * 4 + slot // 2]
        return d // 32, (d // 4) % 8, d % 4

    def spread(src, dst, wait):
        for r in (4, 1, 3, 2, 5, 7, 6):
            q = group_place(r)
            wait.append(remote(src.at[pl.ds(pl.multiple_of(q * 512, 512), 512)], dst.at[p], in_group(r)))
            yield

    def left_chain(h):
        rows = pl.ds(h * 512, 512)
        wait = [
            remote(
                lcand.at[0, 0, rows, pl.ds(pl.multiple_of(((1 - core) * 4 + j) * 128, 128), 128)],
                l_core[h].at[core, j], dev(core_=1 - core),
            )
            for j in range(4)
        ]
        yield
        for c in ld_l[h]:
            c.wait()
        arrive(wait)
        l_half[h] = l_core[h][o_core]
        wait = [remote(l_half.at[h, pl.ds((1 - yhi) * 2, 2)], l_y[h].at[yhi], dev(yhi_=1 - yhi))]
        l_y[h][yhi] = l_half[h, pl.ds(yhi * 2, 2)]
        yield
        arrive(wait)
        for i in range(4):
            l_quar[h, i] = l_y[h][o_yhi, i // 2, (i % 2) * 256:(i % 2) * 256 + 256]
        wait = [remote(l_quar.at[h, flip4(x, r)], l_x[h].at[x], dev(x_=flip4(x, r))) for r in range(1, 4)]
        l_x[h][x] = l_quar[h, x]
        yield
        arrive(wait)
        l_z[h][zlo] = l_x[h][o_x]
        wait = [remote(l_z[h].at[zlo], l_z[h].at[zlo], dev(z_=zpair))]
        yield
        arrive(wait)
        mine = l_all.at[core * 4 + yhi * 2 + x // 2, h, x % 2]
        mine[...] = l_z[h][o_zlo]
        wait = [remote(mine, mine, dev(x_=flip4(x, r))) for r in range(1, 4)]
        yield
        arrive(wait)
        mine = l_all.at[pl.ds(core * 4 + yhi * 2, 2), h]
        wait = [remote(mine, mine, dev(yhi_=1 - yhi))]
        yield
        arrive(wait)
        mine = l_all.at[pl.ds(core * 4, 4), h]
        wait = [remote(mine, mine, dev(core_=1 - core))]
        yield
        arrive(wait)
        yield

    def right_chain(h):
        wait = []
        for r in range(1, 8):
            q = plane_place(r)
            wait.append(remote(
                rcand.at[0, 0, pl.ds(pl.multiple_of((q % 2) * 256 + h * 128, 128), 128),
                         pl.ds(pl.multiple_of((q // 2) * 128, 128), 128)],
                r_one[h].at[ylo * 4 + x], in_plane(r),
            ))
        yield
        ld_r[h].wait()
        arrive(wait)
        for s in range(8):
            oy, oz, ox = right(s)
            r_slot[h, s] = r_one[h][oy * 4 + ox]
        wait = [remote(
            r_slot.at[h, :, pl.ds(pl.multiple_of((1 - zlo) * 64, 64), 64)], r_pair[h].at[zlo],
            dev(z_=(z + 7 + 2 * zlo) % 8),
        )]
        r_pair[h][zlo] = r_slot[h, :, pl.ds(pl.multiple_of(zlo * 64, 64), 64)]
        yield
        arrive(wait)
        for s in range(8):
            oy, oz, ox = right(s)
            r_half[h, s] = r_pair[h][oz % 2, s]
        ring = ((z + 1) // 2) % 4
        wait = [
            remote(
                r_half.at[h, :, pl.ds(pl.multiple_of(((ring + r) % 4) * 16, 16), 16)], r_ring[h].at[ring],
                dev(z_=(z + 2 * r) % 8),
            )
            for r in range(1, 4)
        ]
        r_ring[h][ring] = r_half[h, :, pl.ds(pl.multiple_of(ring * 16, 16), 16)]
        yield
        arrive(wait)
        for s in range(8):
            oy, oz, ox = right(s)
            r_part[h, s // 2, s % 2] = r_ring[h][((oz + 1) // 2) % 4, s]
        wait = [remote(r_part.at[h, flip4(x, r)], r_cols.at[h, x], dev(x_=flip4(x, r))) for r in range(1, 4)]
        r_cols[h, x] = r_part[h, x]
        yield
        arrive(wait)
        sub = zlo * 4 + ring
        wait = [
            remote(
                r_cols.at[h, :, (z + r) % 2], r_all.at[pl.ds(ylo * 4, 4), h, sub], dev(z_=(z + r) % 8),
            )
            for r in range(1, 8)
        ]
        r_all[pl.ds(ylo * 4, 4), h, sub] = r_cols[h, :, zlo]
        yield
        arrive(wait)
        mine = r_all.at[pl.ds(ylo * 4, 4), h]
        wait = [remote(mine, mine, dev(ylo_=1 - ylo))]
        yield
        arrive(wait)
        yield

    def right_basis():
        return jnp.concatenate([r_all[2 * j:2 * j + 2].reshape(512, 128) for j in range(4)], axis=1)

    def turn(src, dst):
        basis = right_basis()

        def one(j, carry):
            cols = jnp.concatenate([src[2 * j], src[2 * j + 1]], axis=1)
            t = lax.dot_general(basis, cols, (((0,), (0,)), ((), ())), preferred_element_type=jnp.float32)
            dst[:, pl.ds(pl.multiple_of(j * 256, 256), 256)] = t.astype(jnp.bfloat16)
            return carry

        lax.fori_loop(0, 4, one, 0)

    def gradient_chain():
        wait = []
        yield from spread(grad, g_in, wait)
        ld_g0.wait()
        arrive(wait)
        turn(g_in, t_g)
        yield

    def moment_chain():
        ld_g.wait()
        ld_f.wait()

        def fold(i, carry):
            rows = pl.ds(pl.multiple_of(i * 256, 256), 256)
            m_send[rows] = (
                beta_first * f_strip[rows] + (1.0 - beta_first) * g_strip[rows].astype(jnp.float32)
            ).astype(jnp.bfloat16)
            return carry

        lax.fori_loop(0, 16, fold, 0)
        m_in[p] = m_send[pl.ds(pl.multiple_of(p * 512, 512), 512)]
        wait = []
        yield from spread(m_send, m_in, wait)
        arrive(wait)
        turn(m_in, t_m)
        yield

    def second_chain():
        ld_s.wait()

        def narrow(i, carry):
            rows = pl.ds(pl.multiple_of(i * 256, 256), 256)
            s_send[rows] = s_strip[rows].astype(jnp.bfloat16)
            return carry

        lax.fori_loop(0, 16, narrow, 0)
        s_in[p] = s_send[pl.ds(pl.multiple_of(p * 512, 512), 512)]
        wait = []
        yield from spread(s_send, s_in, wait)
        arrive(wait)
        yield

    def pair_at(s):
        return (1 - zlo if s >= 2 else zlo) * 2 + (1 - x // 2 if s % 2 else x // 2)

    def left_cols(j):
        return jnp.concatenate(
            [l_all[2 * j].reshape(1024, 128), l_all[2 * j + 1].reshape(1024, 128)], axis=1
        )

    home = pl.ds(pl.multiple_of(p * 512, 512), 512)
    back, back_local = [], []

    def send_home(buf, out, s):
        for r in (2 * s, 2 * s + 1):
            q = group_place(r)
            if r == 0:
                back_local.append(local(buf.at[q], out.at[home]))
            else:
                back.append(remote(buf.at[q], out.at[home], in_group(r)))

    def home_gradient():
        for s in range(4):
            j = pair_at(s)
            g = jnp.dot(t_g[...], left_cols(j), preferred_element_type=jnp.float32)
            gsq[j] = g * g
            low = g.astype(jnp.bfloat16)
            g_send[2 * j] = low[:, :128]
            g_send[2 * j + 1] = low[:, 128:]
            send_home(g_send, grot_out, s)
            yield

    def make_step():
        def left_moment(j, carry):
            m = jnp.dot(t_m[...], left_cols(j), preferred_element_type=jnp.float32)
            old = jnp.concatenate([s_in[2 * j], s_in[2 * j + 1]], axis=1).astype(jnp.float32)
            new = beta_second * old + (1.0 - beta_second) * gsq[j]
            step = m / (correct_first * (jnp.sqrt(new * (1.0 / correct_second)) + epsilon))
            stp[:, pl.ds(pl.multiple_of(j * 256, 256), 256)] = step.astype(jnp.bfloat16)
            return carry

        lax.fori_loop(0, 4, left_moment, 0)
        yield

    def home_update():
        for s in range(4):
            j = pair_at(s)
            rows = jnp.concatenate([l_all[b, j // 2, j % 2] for b in range(8)], axis=1)
            image = lax.dot_general(
                stp[...], rows, (((1,), (1,)), ((), ())), preferred_element_type=jnp.float32
            ).astype(jnp.bfloat16)
            out = jnp.dot(right_basis(), image, preferred_element_type=jnp.float32).astype(jnp.bfloat16)
            u_send[2 * j] = out[:, :128]
            u_send[2 * j + 1] = out[:, 128:]
            send_home(u_send, upd_out, s)
            yield

    g, m, s = gradient_chain(), moment_chain(), second_chain()
    chains = {
        "A": left_chain(0), "B": left_chain(1), "P": right_chain(0), "Q": right_chain(1),
        "g": g, "G": g, "m": m, "M": m, "s": s, "S": s,
        "h": home_gradient(), "w": make_step(), "u": home_update(),
    }
    for name in ORDER:
        next(chains[name])

    arrive(back)
    for c in back_local:
        c.wait()
    for c in sent:
        c.wait_send()


def body(gradient, first_moment, second_moment, left_candidates, right_candidates, left_owner, right_owner):
    bf, f32 = jnp.bfloat16, jnp.float32
    any_, smem = pl.BlockSpec(memory_space=pl.ANY), pl.BlockSpec(memory_space=pltpu.SMEM)
    vm = pltpu.VMEM
    strip = jax.ShapeDtypeStruct(gradient.shape, bf)
    grot, update = pl.pallas_call(
        kernel,
        name="soap_swap",
        out_shape=(strip, strip),
        in_specs=[any_] * 5 + [smem] * 2,
        out_specs=(any_, any_),
        scratch_shapes=[
            vm((4096, 128), bf), vm((4096, 128), f32), vm((4096, 128), f32), vm((4096, 128), bf), vm((4096, 128), bf),
            vm((8, 512, 128), bf), vm((8, 512, 128), bf), vm((8, 512, 128), bf),
            vm((2, 4, 512, 128), bf), vm((2, 4, 256, 128), bf), vm((8, 2, 2, 256, 128), bf),
            vm((2, 8, 128, 128), bf), vm((2, 8, 64, 128), bf), vm((2, 4, 2, 16, 128), bf), vm((2, 4, 2, 16, 128), bf),
            vm((8, 2, 8, 16, 128), bf),
            *[vm((2, 4, 512, 128), bf)] * 2, *[vm((2, 2, 512, 128), bf)] * 2,
            *[vm((4, 256, 128), bf)] * 2, *[vm((2, 256, 128), bf)] * 2,
            *[vm((8, 128, 128), bf)] * 2, *[vm((2, 8, 64, 128), bf)] * 2, *[vm((4, 8, 16, 128), bf)] * 2,
            vm((512, 1024), bf), vm((512, 1024), bf), vm((4, 512, 256), f32), vm((512, 1024), bf),
            vm((8, 512, 128), bf), vm((8, 512, 128), bf),
            pltpu.SemaphoreType.DMA((112,)), pltpu.SemaphoreType.DMA((112,)), pltpu.SemaphoreType.DMA((24,)),
        ],
        compiler_params=pltpu.CompilerParams(
            collective_id=0, has_side_effects=True, vmem_limit_bytes=56 * 2**20
        ),
    )(gradient, first_moment, second_moment, left_candidates, right_candidates, left_owner, right_owner)
    moment_new = beta_first * first_moment + (1.0 - beta_first) * gradient.astype(f32)
    turned = grot.astype(f32)
    second_new = beta_second * second_moment + (1.0 - beta_second) * turned * turned
    return moment_new, second_new, update


def solution(mesh):
    strips = P("tensor", "dp")
    placed = (strips, strips, strips, P("dp", "tensor", None, None), P("dp", "tensor", None, None), P(), P("tensor", None))
    return jax.shard_map(body, mesh=mesh, in_specs=placed, out_specs=(strips,) * 3, check_vma=False)
```

time: 120 us -> 103 us (0.86)
  Pallas kernels: 114 us -> 96.3 us
    pallas_call x1, Pallas kernels: 114 us -> 96.3 us  [body(): pl.pallas_call(kernel, name='soap_swap', out_shape=(strip, strip), in_spe...]
where the time goes in v2:
time: 103 us; the launch traced here: 102 us
  Pallas kernels  96.3 us (93%)
  other arithmetic  3.93 us (4%)
    pallas_call x1, Pallas kernels, body(): pl.pallas_call(kernel, name='soap_swap', out_shape=(strip, strip), in_spe...  96.3 us
    add x1, other arithmetic, body(): beta_second * second_moment + (1.0 - beta_second) * turned * turned  3.93 us

profile of v2, /device:TPU:1, one launch (start us, length us, event | category | flops | bytes accessed | tf_op | source)
XLA Modules:
  0.0 101.9 jit_solution(10609162526955577159)
XLA Ops:
  0.6 0.0 copy-start.1
  0.6 0.0 copy-start
  0.7 0.0 copy-start.2
  0.7 96.3 %soap_swap.1 = (bf16[4096,128]{1,0:T(8,128)(2,1)}, bf16[4096,128]{1,0:T(8,128)(2,1)}) custom-call(bf16[4096,128]{1,0:T(8,128)(2,1)} %grad.1, f32[4096,128]{1,0:T(8,128)} %first.1, f32[4096,128]{1,0:T(8,128)} %second.1, bf16[1,1,1024,1024]{3,2,1,0:T(8,128)(2,1)} %lcand.1, bf16[1,1,512,512]{3,2,1,0:T(8,128)(2,1)} %rcand.1, s32[8]{0:T(128)} %lown.1, s32[1,8]{1,0:T(1,128)} %rown.1), custom_call_target="tpu_custom_call" | custom-call | tf_op jit(solution)/shard_map/soap_swap/pallas_call | solution.py:374
  97.0 0.0 copy-done.1
  97.0 0.0 copy-done
  97.0 0.0 copy-done.2
  97.0 0.0 copy-start.3
  97.0 3.9 %fusion = (f32[4096,128]{1,0:T(8,128)}, f32[4096,128]{1,0:T(8,128)}) fusion(bf16[4096,128]{1,0:T(8,128)(2,1)} %get-tuple-element.5, f32[4096,128]{1,0:T(8,128)S(1)} %copy-done.1, bf16[4096,128]{1,0:T(8,128)(2,1)S(1)} %copy-done.2, f32[4096,128]{1,0:T(8,128)S(1)} %copy-done), kind=kLoop, calls=%fused_computation.1 | loop fusion | flops 4718592 | bytes 10485760 | tf_op jit(solution)/shard_map/add | solution.py:399
  101.0 0.0 copy-done.3
  101.0 1.0 copy.11
Async XLA Ops:
  0.6 96.4 %copy-start.1 = (f32[4096,128]{1,0:T(8,128)S(1)}, f32[4096,128]{1,0:T(8,128)}, u32[]{:S(2)}) copy-start(f32[4096,128]{1,0:T(8,128)} %second.1) | copy-start | bytes 6291460
  0.6 96.4 %copy-start = (f32[4096,128]{1,0:T(8,128)S(1)}, f32[4096,128]{1,0:T(8,128)}, u32[]{:S(2)}) copy-start(f32[4096,128]{1,0:T(8,128)} %first.1) | copy-start | bytes 6291460
  0.7 96.4 %copy-start.2 = (bf16[4096,128]{1,0:T(8,128)(2,1)S(1)}, bf16[4096,128]{1,0:T(8,128)(2,1)}, u32[]{:S(2)}) copy-start(bf16[4096,128]{1,0:T(8,128)(2,1)} %grad.1) | copy-start | bytes 3145732
  97.0 3.9 %copy-start.3 = (bf16[4096,128]{1,0:T(8,128)(2,1)S(1)}, bf16[4096,128]{1,0:T(8,128)(2,1)}, u32[]{:S(2)}) copy-start(bf16[4096,128]{1,0:T(8,128)(2,1)} %get-tuple-element.14) | copy-start | bytes 3145732

commit v3 on v2

--- a/solution.py
+++ b/solution.py
@@ -12,7 +12,7 @@
 correct_second = 1.0 - 0.95**10
 epsilon = 1e-08
 
-ORDER = "PgBsQggmmPBggmAQPgABPQAmBPBAQPgABmQssmAsQsPsmsBAQABGhhhShMwuuuu"
+ORDER = "PQssgAggBgBPggsAQPmQBPABsPBQAssPAmgBmPmQ" + "AsmmQBABmQGAhhShMhwuuuu"
 
 
 def flip4(x, a):
@@ -315,7 +315,7 @@
                 back.append(remote(buf.at[q], out.at[home], in_group(r)))
 
     def home_gradient():
-        for s in range(4):
+        for s in (2, 1, 3, 0):
             j = pair_at(s)
             g = jnp.dot(t_g[...], left_cols(j), preferred_element_type=jnp.float32)
             gsq[j] = g * g
@@ -338,7 +338,7 @@
         yield
 
     def home_update():
-        for s in range(4):
+        for s in (2, 1, 3, 0):
             j = pair_at(s)
             rows = jnp.concatenate([l_all[b, j // 2, j % 2] for b in range(8)], axis=1)
             image = lax.dot_general(

time: 103 us -> 98.8 us (0.959)
  Pallas kernels: 96.3 us -> 93.1 us
    pallas_call x1, Pallas kernels: 96.3 us -> 93.1 us  [body(): pl.pallas_call(kernel, name='soap_swap', out_shape=(strip, strip), in_spe...]
where the time goes in v3:
time: 98.8 us; the launch traced here: 98.7 us
  Pallas kernels  93.1 us (94%)
  other arithmetic  3.93 us (4%)
  local copies, waits for them, and re-layouts  0.99 us (1%)
    pallas_call x1, Pallas kernels, body(): pl.pallas_call(kernel, name='soap_swap', out_shape=(strip, strip), in_spe...  93.1 us
    add x1, other arithmetic, body(): beta_second * second_moment + (1.0 - beta_second) * turned * turned  3.93 us

profile of v3, /device:TPU:1, one launch (start us, length us, event | category | flops | bytes accessed | tf_op | source)
XLA Modules:
  0.0 98.7 jit_solution(4410852963683037525)
XLA Ops:
  0.6 0.0 copy-start.1
  0.6 0.0 copy-start
  0.7 0.0 copy-start.2
  0.7 93.1 %soap_swap.1 = (bf16[4096,128]{1,0:T(8,128)(2,1)}, bf16[4096,128]{1,0:T(8,128)(2,1)}) custom-call(bf16[4096,128]{1,0:T(8,128)(2,1)} %grad.1, f32[4096,128]{1,0:T(8,128)} %first.1, f32[4096,128]{1,0:T(8,128)} %second.1, bf16[1,1,1024,1024]{3,2,1,0:T(8,128)(2,1)} %lcand.1, bf16[1,1,512,512]{3,2,1,0:T(8,128)(2,1)} %rcand.1, s32[8]{0:T(128)} %lown.1, s32[1,8]{1,0:T(1,128)} %rown.1), custom_call_target="tpu_custom_call" | custom-call | tf_op jit(solution)/shard_map/soap_swap/pallas_call | solution.py:374
  93.7 0.0 copy-done.1
  93.7 0.0 copy-done
  93.8 0.0 copy-done.2
  93.8 0.0 copy-start.3
  93.8 3.9 %fusion = (f32[4096,128]{1,0:T(8,128)}, f32[4096,128]{1,0:T(8,128)}) fusion(bf16[4096,128]{1,0:T(8,128)(2,1)} %get-tuple-element.5, f32[4096,128]{1,0:T(8,128)S(1)} %copy-done.1, bf16[4096,128]{1,0:T(8,128)(2,1)S(1)} %copy-done.2, f32[4096,128]{1,0:T(8,128)S(1)} %copy-done), kind=kLoop, calls=%fused_computation.1 | loop fusion | flops 4718592 | bytes 10485760 | tf_op jit(solution)/shard_map/add | solution.py:399
  97.7 0.0 copy-done.3
  97.7 1.0 copy.11
Async XLA Ops:
  0.6 93.1 %copy-start.1 = (f32[4096,128]{1,0:T(8,128)S(1)}, f32[4096,128]{1,0:T(8,128)}, u32[]{:S(2)}) copy-start(f32[4096,128]{1,0:T(8,128)} %second.1) | copy-start | bytes 6291460
  0.6 93.1 %copy-start = (f32[4096,128]{1,0:T(8,128)S(1)}, f32[4096,128]{1,0:T(8,128)}, u32[]{:S(2)}) copy-start(f32[4096,128]{1,0:T(8,128)} %first.1) | copy-start | bytes 6291460
  0.7 93.1 %copy-start.2 = (bf16[4096,128]{1,0:T(8,128)(2,1)S(1)}, bf16[4096,128]{1,0:T(8,128)(2,1)}, u32[]{:S(2)}) copy-start(bf16[4096,128]{1,0:T(8,128)(2,1)} %grad.1) | copy-start | bytes 3145732
  93.8 3.9 %copy-start.3 = (bf16[4096,128]{1,0:T(8,128)(2,1)S(1)}, bf16[4096,128]{1,0:T(8,128)(2,1)}, u32[]{:S(2)}) copy-start(bf16[4096,128]{1,0:T(8,128)(2,1)} %get-tuple-element.14) | copy-start | bytes 3145732

commit v4 on v3

--- a/solution.py
+++ b/solution.py
@@ -315,7 +315,7 @@
                 back.append(remote(buf.at[q], out.at[home], in_group(r)))
 
     def home_gradient():
-        for s in (2, 1, 3, 0):
+        for s in (2, 0, 1, 3):
             j = pair_at(s)
             g = jnp.dot(t_g[...], left_cols(j), preferred_element_type=jnp.float32)
             gsq[j] = g * g
@@ -338,7 +338,7 @@
         yield
 
     def home_update():
-        for s in (2, 1, 3, 0):
+        for s in (2, 0, 1, 3):
             j = pair_at(s)
             rows = jnp.concatenate([l_all[b, j // 2, j % 2] for b in range(8)], axis=1)
             image = lax.dot_general(

time: 98.8 us -> 101 us (1.022); the launches traced: 98.7 us -> 99.8 us
    pallas_call x1, Pallas kernels: 93.1 us -> 94.1 us  [body(): pl.pallas_call(kernel, name='soap_swap', out_shape=(strip, strip), in_spe...]
where the time goes in v4:
time: 101 us; the launch traced here: 99.8 us
  Pallas kernels  94.1 us (93%)
  other arithmetic  3.93 us (4%)
    pallas_call x1, Pallas kernels, body(): pl.pallas_call(kernel, name='soap_swap', out_shape=(strip, strip), in_spe...  94.1 us
    add x1, other arithmetic, body(): beta_second * second_moment + (1.0 - beta_second) * turned * turned  3.93 us

profile of v4, /device:TPU:1, one launch (start us, length us, event | category | flops | bytes accessed | tf_op | source)
XLA Modules:
  0.0 99.8 jit_solution(16464894842990664165)
XLA Ops:
  0.6 0.0 copy-start.1
  0.6 0.0 copy-start
  0.7 0.0 copy-start.2
  0.7 94.1 %soap_swap.1 = (bf16[4096,128]{1,0:T(8,128)(2,1)}, bf16[4096,128]{1,0:T(8,128)(2,1)}) custom-call(bf16[4096,128]{1,0:T(8,128)(2,1)} %grad.1, f32[4096,128]{1,0:T(8,128)} %first.1, f32[4096,128]{1,0:T(8,128)} %second.1, bf16[1,1,1024,1024]{3,2,1,0:T(8,128)(2,1)} %lcand.1, bf16[1,1,512,512]{3,2,1,0:T(8,128)(2,1)} %rcand.1, s32[8]{0:T(128)} %lown.1, s32[1,8]{1,0:T(1,128)} %rown.1), custom_call_target="tpu_custom_call" | custom-call | tf_op jit(solution)/shard_map/soap_swap/pallas_call | solution.py:374
  94.8 0.0 copy-done.1
  94.8 0.0 copy-done
  94.8 0.0 copy-done.2
  94.8 0.0 copy-start.3
  94.8 3.9 %fusion = (f32[4096,128]{1,0:T(8,128)}, f32[4096,128]{1,0:T(8,128)}) fusion(bf16[4096,128]{1,0:T(8,128)(2,1)} %get-tuple-element.5, f32[4096,128]{1,0:T(8,128)S(1)} %copy-done.1, bf16[4096,128]{1,0:T(8,128)(2,1)S(1)} %copy-done.2, f32[4096,128]{1,0:T(8,128)S(1)} %copy-done), kind=kLoop, calls=%fused_computation.1 | loop fusion | flops 4718592 | bytes 10485760 | tf_op jit(solution)/shard_map/add | solution.py:399
  98.8 0.0 copy-done.3
  98.8 1.0 copy.11
Async XLA Ops:
  0.6 94.2 %copy-start.1 = (f32[4096,128]{1,0:T(8,128)S(1)}, f32[4096,128]{1,0:T(8,128)}, u32[]{:S(2)}) copy-start(f32[4096,128]{1,0:T(8,128)} %second.1) | copy-start | bytes 6291460
  0.6 94.2 %copy-start = (f32[4096,128]{1,0:T(8,128)S(1)}, f32[4096,128]{1,0:T(8,128)}, u32[]{:S(2)}) copy-start(f32[4096,128]{1,0:T(8,128)} %first.1) | copy-start | bytes 6291460
  0.7 94.2 %copy-start.2 = (bf16[4096,128]{1,0:T(8,128)(2,1)S(1)}, bf16[4096,128]{1,0:T(8,128)(2,1)}, u32[]{:S(2)}) copy-start(bf16[4096,128]{1,0:T(8,128)(2,1)} %grad.1) | copy-start | bytes 3145732
  94.8 3.9 %copy-start.3 = (bf16[4096,128]{1,0:T(8,128)(2,1)S(1)}, bf16[4096,128]{1,0:T(8,128)(2,1)}, u32[]{:S(2)}) copy-start(bf16[4096,128]{1,0:T(8,128)(2,1)} %get-tuple-element.14) | copy-start | bytes 3145732
